TPU v7x, 128 devices: a whole 4x4x4 slice. The times are simulated.
128 devices in a mesh: blk: 8 (over z, y_hi), tok: 16 (over x, y_lo, core).
Axes of the slice: x: 4, y: 4 (y_hi: 2, y_lo: 2; y = y_hi * 2 + y_lo), z: 4, core: 2. Of those that a mesh axis runs over, the one named last changes fastest.
Arguments:
- inputs: float32 [4096, 16384], P('tok', 'blk'), may hold values from -6 to 6
- first_factor: float32 [16, 1024, 1024], P('blk', 'tok'), may hold values from -0.1875 to 0.1875
- second_factor: float32 [16, 1024, 1024], P('blk', 'tok'), may hold values from -0.1875 to 0.1875
- cotangent: float32 [4096, 16384], P('tok', 'blk'), may hold values from -6 to 6
Outputs:
- input_grad: float32 [4096, 16384], P('tok', 'blk')
- first_grad: float32 [16, 1024, 1024], P('blk', 'tok')
- second_grad: float32 [16, 1024, 1024], P('blk', 'tok')
All inputs are finite; a program needn't handle non-finite values.
Results may differ from a plain program's by a relative error of at most 0.00013.
Values sent between devices are 32-bit elements; how exact they have to be, the bound alone decides.
A program may use at most 128 MiB of HBM per device.

v0:
```python
import math
import jax
import jax.numpy as jnp
from jax import lax
from jax.sharding import PartitionSpec as P


def body(inputs, first_factor, second_factor, cotangent):
    hp = lax.Precision.HIGHEST
    local_blocks = first_factor.shape[0]
    order = first_factor.shape[2]
    blocks = local_blocks * lax.axis_size("blk")
    group = order // blocks
    count = inputs.shape[0]
    xb = inputs.reshape(count, local_blocks, order)
    first_whole, second_whole = (
        lax.all_gather(first_factor, "tok", axis=1, tiled=True),
        lax.all_gather(second_factor, "tok", axis=1, tiled=True),
    )
    first_view = first_whole.reshape(local_blocks, order, blocks, group)
    first = jnp.einsum("tbi,bisg->stbg", xb, first_view, precision=hp).reshape(
        blocks, count, local_blocks * group
    )
    mixed = lax.all_to_all(first, "blk", split_axis=0, concat_axis=2, tiled=True)
    second = jnp.einsum("btk,bko->tbo", mixed, second_whole, precision=hp)
    normal_cdf = 0.5 * (1.0 + jax.scipy.special.erf(second / math.sqrt(2.0)))
    density = jnp.exp(-0.5 * second * second) / math.sqrt(2.0 * math.pi)
    delta_second = cotangent.reshape(count, local_blocks, order) * (normal_cdf + second * density)
    second_grad = jnp.einsum("btk,tbo->bko", mixed, delta_second, precision=hp)
    delta_mixed = jnp.einsum("tbo,bko->btk", delta_second, second_whole, precision=hp)
    delta_first = lax.all_to_all(delta_mixed, "blk", split_axis=2, concat_axis=0, tiled=True)
    delta_view = delta_first.reshape(blocks, count, local_blocks, group)
    first_grad = jnp.einsum("tbi,stbg->bisg", xb, delta_view, precision=hp).reshape(
        local_blocks, order, order
    )
    input_grad = jnp.einsum("stbg,bisg->tbi", delta_view, first_view, precision=hp).reshape(
        count, local_blocks * order
    )
    first_out, second_out = (
        lax.psum_scatter(first_grad, "tok", scatter_dimension=1, tiled=True),
        lax.psum_scatter(second_grad, "tok", scatter_dimension=1, tiled=True),
    )
    return (input_grad, first_out, second_out)


def solution(mesh):
    placed = (P("tok", "blk"), P("blk", "tok", None), P("blk", "tok", None), P("tok", "blk"))
    return jax.shard_map(
        body,
        mesh=mesh,
        in_specs=placed,
        out_specs=(P("tok", "blk"), P("blk", "tok", None), P("blk", "tok", None)),
        check_vma=False,
    )
```

profile of v0, /device:TPU:5, one launch (start us, length us, event | category | flops | bytes accessed | tf_op | source)
XLA Modules:
  0.0 389.0 jit_solution(9547876401872659460)
XLA Ops:
  7.2 0.0 all-gather.3.cloned.1.call-start
  7.2 0.7 all-gather.3.cloned.1.call-update
  7.9 0.0 all-gather.5.cloned.1.call-start
  7.9 0.7 all-gather.5.cloned.1.call-update
  8.6 3.0 reshape.30
  11.7 0.0 copy-start.2
  11.7 52.4 %all-gather.3.cloned.1.call-done = f32[2,1024,1024]{2,1,0:T(8,128)} async-done(((f32[2,64,1024]{2,1,0:T(8,128)}), f32[2,1024,1024]{2,1,0:T(8,128)}) %all-gather.3.cloned.1.call-update) | async-done | bytes 8388624 | tf_op jit(solution)/shard_map/all_gather | solution.py:17
  64.1 8.7 %copy.43 = f32[2,1024,1024]{1,2,0:T(8,128)} copy(f32[2,1024,1024]{2,1,0:T(8,128)} %all-gather.3.cloned.1.call-done) | data formatting | bytes 16777216 | tf_op jit(solution)/shard_map/all_gather | solution.py:17
  72.9 0.0 copy-done.2
  72.9 9.1 %fusion.15 = f32[16,256,2,64]{1,3,0,2:T(8,128)S(1)} fusion(f32[2,1024,16,64]{1,3,2,0:T(8,128)} %bitcast.43, f32[256,2,1024,1]{2,1,0,3:T(2,128)S(1)} %bitcast.46), kind=kOutput, calls=%fused_computation.17 | convolution fusion | flops 6442450944 | bytes 12582912 | tf_op jit(solution)/shard_map/tbi,bisg->stbg/dot_general | solution.py:21
  82.0 1.5 copy.45
  83.6 6.6 %all-to-all-start = ((f32[16,256,128]{1,2,0:T(8,128)}), f32[16,256,128]{1,2,0:T(8,128)S(1)}, u32[]{:S(2)}, u32[]{:S(2)}) async-start(f32[16,256,128]{1,2,0:T(8,128)} %bitcast.49), calls=%async_computation | async-start | bytes 4194304 | tf_op jit(solution)/shard_map/all_to_all | solution.py:24
  90.2 0.2 reduce-scatter.5.cloned.1.call-start
  90.4 2.9 copy.42
  93.3 2.9 copy.48
  96.3 21.9 %all-to-all-done = f32[16,256,128]{1,2,0:T(8,128)S(1)} async-done(((f32[16,256,128]{1,2,0:T(8,128)}), f32[16,256,128]{1,2,0:T(8,128)S(1)}, u32[]{:S(2)}, u32[]{:S(2)}) %all-to-all-start) | async-done | bytes 2097184 | tf_op jit(solution)/shard_map/all_to_all | solution.py:24
  118.2 1.8 copy.47
  120.0 1.7 all_to_all.27
  121.7 15.9 %all-gather.5.cloned.1.call-done = f32[2,1024,1024]{2,1,0:T(8,128)} async-done(((f32[2,64,1024]{2,1,0:T(8,128)}), f32[2,1024,1024]{2,1,0:T(8,128)}) %all-gather.5.cloned.1.call-update) | async-done | bytes 8388624 | tf_op jit(solution)/shard_map/all_gather | solution.py:18
  137.6 10.3 %fusion.6 = f32[256,2,1024]{2,0,1:T(8,128)S(1)} fusion(f32[256,2,1024]{2,0,1:T(8,128)} %copy.48, f32[2,256,1024]{2,1,0:T(8,128)S(1)} %all_to_all.27, f32[2,1024,1024]{2,1,0:T(8,128)} %all-gather.5.cloned.1.call-done), kind=kOutput, calls=%fused_computation.7 | convolution fusion | flops 6447169536 | bytes 14680064 | tf_op jit(solution)/shard_map/btk,bko->tbo/dot_general | solution.py:25
  147.8 0.0 copy-start
  147.8 1.3 copy-done
  149.2 9.0 %fusion.22 = f32[2,1024,1024]{2,1,0:T(8,128)} fusion(f32[2,256,1024]{2,1,0:T(8,128)S(1)} %all_to_all.27, f32[256,2,1024]{2,0,1:T(8,128)S(1)} %fusion.6), kind=kOutput, calls=%fused_computation.20 | convolution fusion | flops 6442450944 | bytes 12582912 | tf_op jit(solution)/shard_map/btk,tbo->bko/dot_general | solution.py:29
  158.1 0.0 copy-start.1
  158.1 0.0 reduce-scatter.5.cloned.1.call-update
  158.1 0.0 reduce-scatter.3.cloned.1.call-start
  158.2 1.5 copy-done.1
  159.7 10.6 %fusion.21 = f32[2,256,1024]{2,1,0:T(8,128)} fusion(f32[256,2,1024]{2,0,1:T(8,128)S(1)} %copy-done.1, f32[2,1024,1024]{2,1,0:T(8,128)} %all-gather.5.cloned.1.call-done), kind=kOutput, calls=%fused_computation.19 | convolution fusion | flops 6442450944 | bytes 12582912 | tf_op jit(solution)/shard_map/tbo,bko->btk/dot_general | solution.py:30
  170.3 2.9 copy.49
  173.1 58.0 %all_to_all.33 = f32[2,256,1024]{1,0,2:T(2,128)S(1)} all-to-all(f32[2,256,1024]{1,0,2:T(2,128)S(1)} %copy.49), channel_id=1, replica_groups=mesh['blk'=8,'tok'=16] {'blk'}, dimensions={2} | all-to-all | bytes 4194304 | tf_op jit(solution)/shard_map/all_to_all | solution.py:31
  231.2 0.2 copy.50
  231.3 0.0 copy-start.3
  231.4 0.1 copy.51
  231.5 1.5 copy-done.3
  233.0 9.2 %fusion.10 = f32[2,16,64,1024]{3,2,1,0:T(8,128)} fusion(f32[16,256,2,64]{1,3,2,0:T(8,128)S(1)} %bitcast.53, f32[256,2,1024,1]{2,1,0,3:T(2,128)S(1)} %bitcast.47), kind=kOutput, calls=%fused_computation.12 | convolution fusion | flops 6442450944 | bytes 12582912 | tf_op jit(solution)/shard_map/tbi,stbg->bisg/dot_general | solution.py:33
  242.2 8.7 %copy.56 = f32[2,1024,1024]{2,1,0:T(8,128)} copy(f32[2,1024,1024]{1,2,0:T(8,128)} %bitcast.45) | data formatting | bytes 16777216 | tf_op jit(solution)/shard_map/reshape | solution.py:33
  250.9 0.0 reduce-scatter.3.cloned.1.call-update
  250.9 10.5 %fusion.18 = f32[256,2,1024]{2,0,1:T(8,128)} fusion(f32[16,256,2,64]{1,3,2,0:T(8,128)S(1)} %bitcast.54, f32[2,1024,16,64]{1,3,2,0:T(8,128)} %bitcast.44), kind=kOutput, calls=%fused_computation.18 | convolution fusion | flops 6442450944 | bytes 12582912 | tf_op jit(solution)/shard_map/stbg,bisg->tbi/dot_general | solution.py:36
  261.4 1.9 copy.53
  263.3 1.8 copy.58
  265.1 15.8 %reduce-scatter.5.cloned.1.call-done = f32[2,64,1024]{2,1,0:T(8,128)} async-done(((f32[2,1024,1024]{2,1,0:T(8,128)}), f32[2,64,1024]{2,1,0:T(8,128)}) %reduce-scatter.5.cloned.1.call-update) | async-done | bytes 524304 | tf_op jit(solution)/shard_map/reduce_scatter | solution.py:41
  280.9 101.6 %reduce-scatter.3.cloned.1.call-done = f32[2,64,1024]{2,1,0:T(8,128)} async-done(((f32[2,1024,1024]{2,1,0:T(8,128)}), f32[2,64,1024]{2,1,0:T(8,128)}) %reduce-scatter.3.cloned.1.call-update) | async-done | bytes 524304 | tf_op jit(solution)/shard_map/reduce_scatter | solution.py:40
Async XLA Ops:
  7.2 57.0 %all-gather.3.cloned.1.call-start = ((), (), s32[]{:S(2)}) async-start(), calls=%async_computation.4 | async-start | bytes 8912896 | tf_op jit(solution)/shard_map/all_gather | solution.py:17
  7.9 129.7 %all-gather.5.cloned.1.call-start = ((), (), s32[]{:S(2)}) async-start(), calls=%async_computation.5 | async-start | bytes 8912896 | tf_op jit(solution)/shard_map/all_gather | solution.py:18
  11.7 61.2 %copy-start.2 = (f32[256,2,1024]{2,1,0:T(2,128)}, f32[256,2,1024]{2,1,0:T(2,128)S(1)}, u32[]{:S(2)}) copy-start(f32[256,2,1024]{2,1,0:T(2,128)S(1)} %reshape.30) | copy-start | bytes 6291460
  83.6 34.6 %all-to-all-start = ((f32[16,256,128]{1,2,0:T(8,128)}), f32[16,256,128]{1,2,0:T(8,128)S(1)}, u32[]{:S(2)}, u32[]{:S(2)}) async-start(f32[16,256,128]{1,2,0:T(8,128)} %bitcast.49), calls=%async_computation | async-start | bytes 4194304 | tf_op jit(solution)/shard_map/all_to_all | solution.py:24
  90.2 190.8 %reduce-scatter.5.cloned.1.call-start = ((), (), s32[]{:S(2)}) async-start(), calls=%async_computation.7 | async-start | bytes 8912896 | tf_op jit(solution)/shard_map/reduce_scatter | solution.py:41
  147.8 1.3 copy-start
  158.1 1.6 copy-start.1
  158.1 224.4 %reduce-scatter.3.cloned.1.call-start = ((), (), s32[]{:S(2)}) async-start(), calls=%async_computation.6 | async-start | bytes 8912896 | tf_op jit(solution)/shard_map/reduce_scatter | solution.py:40
  231.3 1.6 copy-start.3
Sparse Core Ops, SparseCore 0:
  9.7 54.4 all-gather.2
  65.8 71.7 all-gather.4
  158.3 122.6 reduce-scatter.4
  283.7 98.7 reduce-scatter.2
where the time goes:
time: 390 us; the launch traced here: 389 us
  waiting for transfers between devices  209 us (54%)
  matrix products  58.6 us (15%)
  blocking collectives  58 us (15%)
  local copies, waits for them, and re-layouts  42.6 us (11%)
  between operations  13.9 us (4%)
  starting transfers between devices  6.94 us (2%)
    reduce_scatter x1, waiting for transfers between devices, body(): lax.psum_scatter(first_grad, 'tok', scatter_dimension=1, tiled=True)  102 us
    all_to_all x1, blocking collectives, body(): lax.all_to_all(delta_mixed, 'blk', split_axis=2, concat_axis=0, tiled=True)  58 us
    all_gather x1, waiting for transfers between devices, body(): lax.all_gather(first_factor, 'tok', axis=1, tiled=True)  52.4 us
    all_to_all x1, waiting for transfers between devices, body(): lax.all_to_all(first, 'blk', split_axis=0, concat_axis=2, tiled=True)  21.9 us
    all_gather x1, waiting for transfers between devices, body(): lax.all_gather(second_factor, 'tok', axis=1, tiled=True)  15.9 us
    reduce_scatter x1, waiting for transfers between devices, body(): lax.psum_scatter(second_grad, 'tok', scatter_dimension=1, tiled=True)  15.8 us
    dot_general x1, matrix products, body(): jnp.einsum('tbo,bko->btk', delta_second, second_whole, precision=hp)  10.6 us
    dot_general x1, matrix products, body(): jnp.einsum('stbg,bisg->tbi', delta_view, first_view, precision=hp)  10.5 us
  transfers between devices with their start and end apart: 5, of which 5 were waited for; matrix products, arithmetic and copies ran while one was open for 20% of the time, Pallas kernels for 0%

commit v1 on v0

--- a/solution.py
+++ b/solution.py
@@ -15,7 +15,9 @@
     xb = inputs.reshape(count, local_blocks, order)
     first_whole, second_whole = (
         lax.all_gather(first_factor, "tok", axis=1, tiled=True),
-        lax.all_gather(second_factor, "tok", axis=1, tiled=True),
+        jnp.concatenate(
+            lax.all_to_all(jnp.stack([second_factor] * lax.axis_size("tok")), "tok", 0, 0), axis=1
+        ),
     )
     first_view = first_whole.reshape(local_blocks, order, blocks, group)
     first = jnp.einsum("tbi,bisg->stbg", xb, first_view, precision=hp).reshape(

time: 390 us -> 477 us (1.22)
  waiting for transfers between devices: 209 us -> 277 us
  local copies, waits for them, and re-layouts: 42.6 us -> 56.1 us
    all_gather x1, waiting for transfers between devices: 52.4 us -> 140 us  [body(): lax.all_gather(first_factor, 'tok', axis=1, tiled=True)]
    all_gather x1 -> x0, waiting for transfers between devices: 15.9 us -> none  [body(): lax.all_gather(second_factor, 'tok', axis=1, tiled=True)]
    reshape x0 -> x1, local copies, waits for them, and re-layouts: none -> 8.26 us  [body(): jnp.concatenate(lax.all_to_all(jnp.stack([second_factor] * lax.axis_size(...]
    all_to_all x1, waiting for transfers between devices: 21.9 us -> 13.7 us  [body(): lax.all_to_all(first, 'blk', split_axis=0, concat_axis=2, tiled=True)]
    all_to_all x0 -> x1, starting transfers between devices: none -> 6.15 us  [body(): lax.all_to_all(jnp.stack([second_factor] * lax.axis_size('tok')), 'tok',...]
    reduce_scatter x1, waiting for transfers between devices: 15.8 us -> 21.4 us  [body(): lax.psum_scatter(second_grad, 'tok', scatter_dimension=1, tiled=True)]
    another operation x0 -> x1, local copies, waits for them, and re-layouts: none -> 5.32 us  [body(): jnp.stack([second_factor] * lax.axis_size('tok'))]
  transfers between devices with their start and end apart: 5 -> 5, of which waited for: 5 -> 4; matrix products, arithmetic and copies ran while one was open for 20% -> 18% of each run, Pallas kernels for 0% -> 0%
where the time goes in v1:
time: 477 us; the launch traced here: 476 us
  waiting for transfers between devices  277 us (58%)
  matrix products  58.6 us (12%)
  blocking collectives  58.5 us (12%)
  local copies, waits for them, and re-layouts  56.1 us (12%)
  between operations  13.8 us (3%)
  starting transfers between devices  11.4 us (2%)
    all_gather x1, waiting for transfers between devices, body(): lax.all_gather(first_factor, 'tok', axis=1, tiled=True)  140 us
    reduce_scatter x1, waiting for transfers between devices, body(): lax.psum_scatter(first_grad, 'tok', scatter_dimension=1, tiled=True)  101 us
    all_to_all x1, blocking collectives, body(): lax.all_to_all(delta_mixed, 'blk', split_axis=2, concat_axis=0, tiled=True)  58.5 us
    reduce_scatter x1, waiting for transfers between devices, body(): lax.psum_scatter(second_grad, 'tok', scatter_dimension=1, tiled=True)  21.4 us
    all_to_all x1, waiting for transfers between devices, body(): lax.all_to_all(first, 'blk', split_axis=0, concat_axis=2, tiled=True)  13.7 us
    dot_general x1, matrix products, body(): jnp.einsum('tbo,bko->btk', delta_second, second_whole, precision=hp)  10.6 us
    dot_general x1, matrix products, body(): jnp.einsum('stbg,bisg->tbi', delta_view, first_view, precision=hp)  10.5 us
    dot_general x1, matrix products, body(): second = jnp.einsum('btk,bko->tbo', mixed, second_whole, precision=hp)  10.3 us
  transfers between devices with their start and end apart: 5, of which 4 were waited for; matrix products, arithmetic and copies ran while one was open for 18% of the time, Pallas kernels for 0%

profile of v1, /device:TPU:5, one launch (start us, length us, event | category | flops | bytes accessed | tf_op | source)
XLA Modules:
  0.0 475.9 jit_solution(2600200399602610627)
XLA Ops:
  7.2 0.0 all-gather.2.cloned.1.call-start
  7.2 0.7 all-gather.2.cloned.1.call-update
  7.9 5.3 %stack.2 = f32[16,2,64,1024]{3,2,1,0:T(8,128)} broadcast(f32[2,64,1024]{2,1,0:T(8,128)} %param.6), dimensions={1,2,3} | broadcast | bytes 8912896 | tf_op jit(solution)/shard_map/stack | solution.py:19
  13.2 6.1 %all-to-all-start.1 = ((f32[16,2,64,1024]{3,2,1,0:T(8,128)}), f32[16,2,64,1024]{3,2,1,0:T(8,128)}, u32[]{:S(2)}, u32[]{:S(2)}) async-start(f32[16,2,64,1024]{3,2,1,0:T(8,128)} %stack.2), calls=%async_computation.1 | async-start | bytes 16777216 | tf_op jit(solution)/shard_map/all_to_all | solution.py:19
  19.4 3.0 reshape.38
  22.4 0.0 copy-start.2
  22.4 140.2 %all-gather.2.cloned.1.call-done = f32[2,1024,1024]{2,1,0:T(8,128)} async-done(((f32[2,64,1024]{2,1,0:T(8,128)}), f32[2,1024,1024]{2,1,0:T(8,128)}) %all-gather.2.cloned.1.call-update) | async-done | bytes 8388624 | tf_op jit(solution)/shard_map/all_gather | solution.py:17
  162.7 8.7 %copy.44 = f32[2,1024,1024]{1,2,0:T(8,128)} copy(f32[2,1024,1024]{2,1,0:T(8,128)} %all-gather.2.cloned.1.call-done) | data formatting | bytes 16777216 | tf_op jit(solution)/shard_map/all_gather | solution.py:17
  171.4 0.0 copy-done.2
  171.4 9.2 %fusion.15 = f32[16,256,2,64]{1,3,0,2:T(8,128)S(1)} fusion(f32[2,1024,16,64]{1,3,2,0:T(8,128)} %bitcast.47, f32[256,2,1024,1]{2,1,0,3:T(2,128)S(1)} %bitcast.50), kind=kOutput, calls=%fused_computation.17 | convolution fusion | flops 6442450944 | bytes 12582912 | tf_op jit(solution)/shard_map/tbi,bisg->stbg/dot_general | solution.py:23
  180.6 1.6 copy.46
  182.1 0.0 all-to-all-done.1
  182.2 4.8 %all-to-all-start = ((f32[16,256,128]{1,2,0:T(8,128)}), f32[16,256,128]{1,2,0:T(8,128)S(1)}, u32[]{:S(2)}, u32[]{:S(2)}) async-start(f32[16,256,128]{1,2,0:T(8,128)} %bitcast.4), calls=%async_computation | async-start | bytes 4194304 | tf_op jit(solution)/shard_map/all_to_all | solution.py:26
  186.9 0.2 reduce-scatter.5.cloned.1.call-start
  187.1 2.9 copy.43
  190.0 2.9 copy.50
  192.9 8.3 %copy.49 = f32[2,16,64,1024]{3,2,1,0:T(8,128)} copy(f32[2,16,64,1024]{3,2,0,1:T(8,128)} %bitcast.8) | data formatting | bytes 16777216 | tf_op jit(solution)/shard_map/reshape | solution.py:18
  201.2 13.7 %all-to-all-done = f32[16,256,128]{1,2,0:T(8,128)S(1)} async-done(((f32[16,256,128]{1,2,0:T(8,128)}), f32[16,256,128]{1,2,0:T(8,128)S(1)}, u32[]{:S(2)}, u32[]{:S(2)}) %all-to-all-start) | async-done | bytes 2097184 | tf_op jit(solution)/shard_map/all_to_all | solution.py:26
  214.9 1.8 copy.48
  216.7 1.7 all_to_all.30
  218.4 10.3 %fusion.6 = f32[256,2,1024]{2,0,1:T(8,128)S(1)} fusion(f32[256,2,1024]{2,0,1:T(8,128)} %copy.50, f32[2,256,1024]{2,1,0:T(8,128)S(1)} %all_to_all.30, f32[2,1024,1024]{2,1,0:T(8,128)} %bitcast.45), kind=kOutput, calls=%fused_computation.7 | convolution fusion | flops 6447169536 | bytes 14680064 | tf_op jit(solution)/shard_map/btk,bko->tbo/dot_general | solution.py:27
  228.7 0.0 copy-start
  228.7 1.3 copy-done
  230.0 8.9 %fusion.22 = f32[2,1024,1024]{2,1,0:T(8,128)} fusion(f32[2,256,1024]{2,1,0:T(8,128)S(1)} %all_to_all.30, f32[256,2,1024]{2,0,1:T(8,128)S(1)} %fusion.6), kind=kOutput, calls=%fused_computation.20 | convolution fusion | flops 6442450944 | bytes 12582912 | tf_op jit(solution)/shard_map/btk,tbo->bko/dot_general | solution.py:31
  239.0 0.0 copy-start.1
  239.0 0.0 reduce-scatter.5.cloned.1.call-update
  239.0 0.3 reduce-scatter.3.cloned.1.call-start
  239.3 1.3 copy-done.1
  240.6 10.6 %fusion.21 = f32[2,256,1024]{2,1,0:T(8,128)} fusion(f32[256,2,1024]{2,0,1:T(8,128)S(1)} %copy-done.1, f32[2,1024,1024]{2,1,0:T(8,128)} %bitcast.46), kind=kOutput, calls=%fused_computation.19 | convolution fusion | flops 6442450944 | bytes 12582912 | tf_op jit(solution)/shard_map/tbo,bko->btk/dot_general | solution.py:32
  251.1 2.8 copy.51
  254.0 58.5 %all_to_all.38 = f32[2,256,1024]{1,0,2:T(2,128)S(1)} all-to-all(f32[2,256,1024]{1,0,2:T(2,128)S(1)} %copy.51), channel_id=1, replica_groups=mesh['blk'=8,'tok'=16] {'blk'}, dimensions={2} | all-to-all | bytes 4194304 | tf_op jit(solution)/shard_map/all_to_all | solution.py:33
  312.5 0.2 copy.52
  312.7 0.0 copy-start.3
  312.7 0.1 copy.53
  312.9 1.5 copy-done.3
  314.3 9.2 %fusion.10 = f32[2,16,64,1024]{3,2,1,0:T(8,128)} fusion(f32[16,256,2,64]{1,3,2,0:T(8,128)S(1)} %bitcast.56, f32[256,2,1024,1]{2,1,0,3:T(2,128)S(1)} %bitcast.51), kind=kOutput, calls=%fused_computation.12 | convolution fusion | flops 6442450944 | bytes 12582912 | tf_op jit(solution)/shard_map/tbi,stbg->bisg/dot_general | solution.py:35
  323.5 8.8 %copy.58 = f32[2,1024,1024]{2,1,0:T(8,128)} copy(f32[2,1024,1024]{1,2,0:T(8,128)} %bitcast.49) | data formatting | bytes 16777216 | tf_op jit(solution)/shard_map/reshape | solution.py:35
  332.3 0.0 reduce-scatter.3.cloned.1.call-update
  332.3 10.5 %fusion.18 = f32[256,2,1024]{2,0,1:T(8,128)} fusion(f32[16,256,2,64]{1,3,2,0:T(8,128)S(1)} %bitcast.57, f32[2,1024,16,64]{1,3,2,0:T(8,128)} %bitcast.48), kind=kOutput, calls=%fused_computation.18 | convolution fusion | flops 6442450944 | bytes 12582912 | tf_op jit(solution)/shard_map/stbg,bisg->tbi/dot_general | solution.py:38
  342.8 1.9 copy.55
  344.8 1.8 copy.60
  346.6 21.4 %reduce-scatter.5.cloned.1.call-done = f32[2,64,1024]{2,1,0:T(8,128)} async-done(((f32[2,1024,1024]{2,1,0:T(8,128)}), f32[2,64,1024]{2,1,0:T(8,128)}) %reduce-scatter.5.cloned.1.call-update) | async-done | bytes 524304 | tf_op jit(solution)/shard_map/reduce_scatter | solution.py:43
  368.0 101.4 %reduce-scatter.3.cloned.1.call-done = f32[2,64,1024]{2,1,0:T(8,128)} async-done(((f32[2,1024,1024]{2,1,0:T(8,128)}), f32[2,64,1024]{2,1,0:T(8,128)}) %reduce-scatter.3.cloned.1.call-update) | async-done | bytes 524304 | tf_op jit(solution)/shard_map/reduce_scatter | solution.py:42
Async XLA Ops:
  7.2 155.5 %all-gather.2.cloned.1.call-start = ((), (), s32[]{:S(2)}) async-start(), calls=%async_computation.5 | async-start | bytes 8912896 | tf_op jit(solution)/shard_map/all_gather | solution.py:17
  13.2 168.9 %all-to-all-start.1 = ((f32[16,2,64,1024]{3,2,1,0:T(8,128)}), f32[16,2,64,1024]{3,2,1,0:T(8,128)}, u32[]{:S(2)}, u32[]{:S(2)}) async-start(f32[16,2,64,1024]{3,2,1,0:T(8,128)} %stack.2), calls=%async_computation.1 | async-start | bytes 16777216 | tf_op jit(solution)/shard_map/all_to_all | solution.py:19
  22.4 149.0 %copy-start.2 = (f32[256,2,1024]{2,1,0:T(2,128)}, f32[256,2,1024]{2,1,0:T(2,128)S(1)}, u32[]{:S(2)}) copy-start(f32[256,2,1024]{2,1,0:T(2,128)S(1)} %reshape.38) | copy-start | bytes 6291460
  182.2 32.8 %all-to-all-start = ((f32[16,256,128]{1,2,0:T(8,128)}), f32[16,256,128]{1,2,0:T(8,128)S(1)}, u32[]{:S(2)}, u32[]{:S(2)}) async-start(f32[16,256,128]{1,2,0:T(8,128)} %bitcast.4), calls=%async_computation | async-start | bytes 4194304 | tf_op jit(solution)/shard_map/all_to_all | solution.py:26
  186.9 181.1 %reduce-scatter.5.cloned.1.call-start = ((), (), s32[]{:S(2)}) async-start(), calls=%async_computation.7 | async-start | bytes 8912896 | tf_op jit(solution)/shard_map/reduce_scatter | solution.py:43
  228.7 1.3 copy-start
  239.0 1.6 copy-start.1
  239.0 230.3 %reduce-scatter.3.cloned.1.call-start = ((), (), s32[]{:S(2)}) async-start(), calls=%async_computation.6 | async-start | bytes 8912896 | tf_op jit(solution)/shard_map/reduce_scatter | solution.py:42
  312.7 1.6 copy-start.3
Sparse Core Ops, SparseCore 0:
  9.7 152.9 all-gather.1
  239.1 128.8 reduce-scatter.4
  371.0 98.3 reduce-scatter.2
